TPU v7x, 32 devices: a whole 2x2x4 slice. The times are simulated.
32 devices in a mesh: parts: 2 (over y), tensor: 2 (over x), dp: 8 (over z, core).
Axes of the slice: x: 2, y: 2, z: 4, core: 2. Of those that a mesh axis runs over, the one named last changes fastest.
Arguments:
- activations: bfloat16 [48, 512, 28672], P(('parts', 'dp'), None, 'tensor'), parts along dimension 0, may hold values from -6 to 6
- out_grads: bfloat16 [48, 512, 8192], P(('parts', 'dp'), None, 'tensor'), parts along dimension 0, may hold values from -6 to 6
- proj_in: bfloat16 [28672, 64], P('tensor'), may hold values from -0.03125 to 0.03125
- proj_out: bfloat16 [8192, 64], P('tensor'), may hold values from -0.0625 to 0.0625
- fisher_prior: float32 [4096, 4096], P('tensor'), as said below
- test_grads: float32 [256, 4096], P(('parts', 'dp')), parts along dimension 0, may hold values from -6 to 6
Outputs:
- scores: float32 [48, 128], P(('parts', 'dp')), parts along dimension 0
- preconditioned: float32 [256, 4096], P('parts', 'tensor'), parts along dimension 0
There are 2 independent parts, one for each index of `parts`. A program takes and returns all parts, laid end to end along the dimension named above; an argument that names none is the same for every part. Nothing has to cross between parts.
Inputs may be any that keep to these rules, and one draw needn't show every extreme that they name: `fisher_prior`: the prior is symmetric.
All inputs are finite; a program needn't handle non-finite values.
Results may differ from a plain program's by a relative error of at most 0.0003.
Values sent between devices are 32-bit elements; how exact they have to be, the bound alone decides.
A program may use at most 320 MiB of HBM per device.

v0:
```python
import jax
import jax.numpy as jnp
from jax import lax
from jax.sharding import PartitionSpec as P

LEN = 512
ITERS = 4


DAMPING = 0.1
CONTRACT = (((1,), (1,)), ((), ()))


def project_grads(paired):
    rank_dim = paired.shape[2] // 2
    products = jnp.einsum(
        "eto,eti->eoi",
        paired[:, :, :rank_dim],
        paired[:, :, rank_dim:],
        precision=lax.Precision.HIGHEST,
    )
    return products.reshape(products.shape[0], -1) / LEN


def shards(activations, out_grads, proj_in, proj_out, fisher_prior, test_grads):
    batch_rows, length_tok, width_ff = activations.shape
    width_model = out_grads.shape[2]
    act_part = jnp.dot(
        activations.reshape(-1, width_ff), proj_in, preferred_element_type=jnp.float32
    ).reshape(batch_rows, length_tok, -1)
    grad_part = jnp.dot(
        out_grads.reshape(-1, width_model), proj_out, preferred_element_type=jnp.float32
    ).reshape(batch_rows, length_tok, -1)
    paired = jnp.concatenate([grad_part, act_part], axis=2)
    summed = lax.psum(paired, "tensor")
    gradients = project_grads(summed)
    rows_here = fisher_prior.shape[0]
    offset = lax.axis_index("tensor") * rows_here
    tests = lax.all_gather(test_grads, "dp", axis=0, tiled=True)
    own_grads = lax.dynamic_slice_in_dim(gradients, offset, rows_here, 1)
    batch_fisher = jnp.dot(own_grads.T, gradients, precision=lax.Precision.HIGHEST)
    fisher_rows = fisher_prior + lax.psum(batch_fisher, "dp")
    residual = lax.dynamic_slice_in_dim(tests, offset, rows_here, 1)
    direction = residual
    solution = jnp.zeros_like(residual)
    norm_now = jnp.sum(tests * tests, axis=1)
    width_low = 1
    for iteration in range(ITERS):
        start_acc = (
            jnp.zeros_like(direction),
            jnp.zeros((direction.shape[0], width_low), jnp.float32),
        )
        image_acc = lax.dot_general(
            lax.all_gather(direction, "tensor", axis=1, tiled=True),
            fisher_rows,
            CONTRACT,
            precision=lax.Precision.HIGHEST,
        )
        coeffs = start_acc[1]
        image_acc, coeffs = (image_acc, coeffs)
        applied = image_acc + DAMPING * direction
        curve = lax.psum(jnp.sum(direction * applied, axis=1), "tensor")
        step_size = norm_now / curve
        solution = solution + step_size[:, None] * direction
        residual = residual - step_size[:, None] * applied
        if iteration + 1 < ITERS:
            norm_next = lax.psum(jnp.sum(residual * residual, axis=1), "tensor")
            direction = residual + (norm_next / norm_now)[:, None] * direction
            norm_now = norm_next
    own_grads = lax.dynamic_slice_in_dim(gradients, offset, rows_here, 1)
    partial_scores = jnp.dot(own_grads, solution.T, precision=lax.Precision.HIGHEST)
    scores = lax.psum(partial_scores, "tensor")
    return (scores, solution)


def solution(mesh):
    return jax.shard_map(
        shards,
        mesh=mesh,
        in_specs=(
            P(("parts", "dp"), None, "tensor"),
            P(("parts", "dp"), None, "tensor"),
            P("tensor", None),
            P("tensor", None),
            P("tensor", None),
            P(("parts", "dp"), None),
        ),
        out_specs=(P(("parts", "dp"), None), P("parts", "tensor")),
        check_vma=False,
    )
```

profile of v0, /device:TPU:0, one launch (start us, length us, event | category | flops | bytes accessed | tf_op | source)
XLA Modules:
  0.0 1115.4 jit_solution(7795184679056968451)
XLA Ops:
  8.1 1.4 copy-done
  9.5 20.9 %fusion.1 = f32[3,512,64]{1,2,0:T(8,128)S(1)} fusion(bf16[3,512,14336]{2,1,0:T(8,128)(2,1)} %param.6, bf16[14336,64]{0,1:T(8,128)(2,1)S(1)} %copy-done), kind=kOutput, calls=%fused_computation.6 | convolution fusion | flops 2818572288 | bytes 46268416 | tf_op jit(solution)/shard_map/dot_general | solution.py:28
  30.4 8.5 fusion.4
  40.7 36.4 %all-reduce.3.cloned.1.call-done = f32[3,512,128]{1,2,0:T(8,128)} async-done(((f32[3,512,128]{1,2,0:T(8,128)}), f32[3,512,128]{1,2,0:T(8,128)}) %all-reduce.3.cloned.1.call-update) | async-done | bytes 786448 | tf_op jit(solution)/shard_map/psum | solution.py:35
  77.0 1.6 convolution_multiply_fusion
  78.7 30.2 %fusion.10 = f32[2048,4096]{1,0:T(8,128)} fusion(f32[3,4096]{1,0:T(4,128)S(1)} %div.31, s32[]{:T(128)S(6)} %select_n.2), kind=kOutput, calls=%fused_computation.30 | convolution fusion | flops 301989888 | bytes 33652740 | tf_op jit(solution)/shard_map/dot_general | solution.py:41
  109.0 2.3 constant_dynamic-slice_fusion
  111.7 1.8 multiply_reduce_fusion
  113.5 643.9 %all-reduce.5.cloned.1.call-done = f32[2048,4096]{1,0:T(8,128)} async-done(((f32[2048,4096]{1,0:T(8,128)}), f32[2048,4096]{1,0:T(8,128)}) %all-reduce.5.cloned.1.call-update) | async-done | bytes 33554448 | tf_op jit(solution)/shard_map/psum | solution.py:42
  757.4 33.5 %add.59 = f32[2048,4096]{1,0:T(8,128)} add(f32[2048,4096]{1,0:T(8,128)} %param.10, f32[2048,4096]{1,0:T(8,128)} %all-reduce.5.cloned.1.call-done) | non-fusion elementwise | flops 8388608 | bytes 100663296 | tf_op jit(solution)/shard_map/add | solution.py:42
  790.9 39.5 %multiply_reduce_fusion.6 = (f32[128]{0:T(128)S(1)}, f32[128,2048]{1,0:T(8,128)S(1)}) fusion(f32[128,2048]{1,0:T(8,128)S(1)} %copy-done.5, f32[128,4096]{1,0:T(8,128)} %all-gather.8.cloned.1.call-done, f32[2048,4096]{1,0:T(8,128)} %add.59), kind=kOutput, calls=%fused_computation.22 | convolution fusion | flops 12885950464 | bytes 37749248 | tf_op jit(solution)/shard_map/dot_general | solution.py:53
  830.3 4.9 psum.72
  835.3 1.5 multiply_reduce_fusion.5
  836.8 4.9 psum.73
  841.7 2.5 multiply_add_fusion.3
  844.8 32.6 %all-gather.10.cloned.1.call-done = f32[128,4096]{1,0:T(8,128)} async-done(((f32[128,2048]{1,0:T(8,128)}), f32[128,4096]{1,0:T(8,128)}) %all-gather.10.cloned.1.call-update) | async-done | bytes 2097168 | tf_op jit(solution)/shard_map/all_gather | solution.py:54
  877.4 40.2 %multiply_reduce_fusion.4 = (f32[128]{0:T(128)S(1)}, f32[128,2048]{1,0:T(8,128)}) fusion(f32[128,2048]{1,0:T(8,128)} %multiply_add_fusion.3, f32[128,4096]{1,0:T(8,128)} %all-gather.10.cloned.1.call-done, f32[2048,4096]{1,0:T(8,128)} %add.59), kind=kOutput, calls=%fused_computation.18 | convolution fusion | flops 12885950464 | bytes 37749248 | tf_op jit(solution)/shard_map/dot_general | solution.py:53
  917.6 4.9 psum.74
  922.5 2.9 multiply_reduce_fusion.3
  925.4 4.9 psum.75
  930.3 2.4 multiply_add_fusion.2
  933.0 33.0 %all-gather.12.cloned.1.call-done = f32[128,4096]{1,0:T(8,128)} async-done(((f32[128,2048]{1,0:T(8,128)}), f32[128,4096]{1,0:T(8,128)}) %all-gather.12.cloned.1.call-update) | async-done | bytes 2097168 | tf_op jit(solution)/shard_map/all_gather | solution.py:54
  966.0 40.2 %multiply_reduce_fusion.2 = (f32[128]{0:T(128)S(1)}, f32[128,2048]{1,0:T(8,128)}) fusion(f32[128,2048]{1,0:T(8,128)} %multiply_add_fusion.2, f32[128,4096]{1,0:T(8,128)} %all-gather.12.cloned.1.call-done, f32[2048,4096]{1,0:T(8,128)} %add.59), kind=kOutput, calls=%fused_computation.14 | convolution fusion | flops 12885950464 | bytes 37749248 | tf_op jit(solution)/shard_map/dot_general | solution.py:53
  1006.2 5.1 psum.76
  1011.3 1.5 multiply_reduce_fusion.1
  1012.8 5.2 psum.77
  1018.0 2.5 multiply_add_fusion.1
  1020.5 33.3 %all-gather.14.cloned.1.call-done = f32[128,4096]{1,0:T(8,128)} async-done(((f32[128,2048]{1,0:T(8,128)}), f32[128,4096]{1,0:T(8,128)}) %all-gather.14.cloned.1.call-update) | async-done | bytes 2097168 | tf_op jit(solution)/shard_map/all_gather | solution.py:54
  1053.8 39.5 %fusion.3 = f32[128]{0:T(128)S(1)} fusion(f32[128,2048]{1,0:T(8,128)} %multiply_add_fusion.1, f32[128,4096]{1,0:T(8,128)} %all-gather.14.cloned.1.call-done, f32[2048,4096]{1,0:T(8,128)} %add.59), kind=kOutput, calls=%fused_computation.8 | convolution fusion | flops 12885950464 | bytes 36700672 | tf_op jit(solution)/shard_map/dot_general | solution.py:53
  1093.3 4.9 psum.78
  1098.3 2.3 multiply_add_fusion
  1102.5 5.5 psum.79
  (41 shorter events, 5.0 us)
Async XLA Ops:
  8.0 1.5 copy-start
  8.0 22.4 %copy-start.7 = (bf16[4096,64]{0,1:T(8,128)(2,1)S(1)}, bf16[4096,64]{0,1:T(8,128)(2,1)}, u32[]{:S(2)}) copy-start(bf16[4096,64]{0,1:T(8,128)(2,1)} %param.9) | copy-start | bytes 1572868
  8.0 69.0 %all-reduce.3.cloned.1.call-start = ((), (), s32[]{:S(2)}) async-start(), calls=%async_computation | async-start | bytes 1572864 | tf_op jit(solution)/shard_map/psum | solution.py:35
  39.8 69.2 %all-gather.6.cloned.1.call-start = ((), (), s32[]{:S(2)}) async-start(), calls=%async_computation.1 | async-start | bytes 2359296 | tf_op jit(solution)/shard_map/all_gather | solution.py:39
  40.4 717.0 %all-reduce.5.cloned.1.call-start = ((), (), s32[]{:S(2)}) async-start(), calls=%async_computation.3 | async-start | bytes 67108864 | tf_op jit(solution)/shard_map/psum | solution.py:42
  109.0 681.9 %all-gather.8.cloned.1.call-start = ((), (), s32[]{:S(2)}) async-start(), calls=%async_computation.2 | async-start | bytes 3145728 | tf_op jit(solution)/shard_map/all_gather | solution.py:54
  111.4 766.0 %all-gather.10.cloned.1.call-start = ((), (), s32[]{:S(2)}) async-start(), calls=%async_computation.4 | async-start | bytes 3145728 | tf_op jit(solution)/shard_map/all_gather | solution.py:54
  113.5 677.4 %copy-start.5 = (f32[128,2048]{1,0:T(8,128)S(1)}, f32[128,2048]{1,0:T(8,128)}, u32[]{:S(2)}) copy-start(f32[128,2048]{1,0:T(8,128)} %constant_dynamic-slice_fusion) | copy-start | bytes 3145732
  844.3 121.7 %all-gather.12.cloned.1.call-start = ((), (), s32[]{:S(2)}) async-start(), calls=%async_computation.5 | async-start | bytes 3145728 | tf_op jit(solution)/shard_map/all_gather | solution.py:54
  922.5 7.8 copy-start.3
  932.7 78.5 %copy-start.4 = (f32[128,2048]{1,0:T(8,128)S(1)}, f32[128,2048]{1,0:T(8,128)}, u32[]{:S(2)}) copy-start(f32[128,2048]{1,0:T(8,128)} %get-tuple-element.3) | copy-start | bytes 3145732
  932.8 121.0 %all-gather.14.cloned.1.call-start = ((), (), s32[]{:S(2)}) async-start(), calls=%async_computation.6 | async-start | bytes 3145728 | tf_op jit(solution)/shard_map/all_gather | solution.py:54
  1006.2 11.7 %copy-start.2 = (f32[128,2048]{1,0:T(8,128)S(1)}, f32[128,2048]{1,0:T(8,128)}, u32[]{:S(2)}) copy-start(f32[128,2048]{1,0:T(8,128)} %multiply_add_fusion.2) | copy-start | bytes 3145732
  1098.3 9.7 copy-start.1
  1100.6 1.0 copy-start.6
Sparse Core Ops, SparseCore 0:
  40.0 37.0 all-reduce.2
  112.0 33.1 all-gather.7
  844.4 32.9 all-gather.9
  932.9 33.1 all-gather.11
  1020.6 33.1 all-gather.13
Sparse Core Ops, SparseCore 1:
  41.9 31.7 all-gather.5
  109.0 648.3 all-reduce.4
where the time goes:
time: 1120 us
  waiting for transfers between devices  780 us (70%)
  matrix products  221 us (20%)
  other arithmetic  52 us (5%)
  blocking collectives  40.4 us (4%)
  between operations  15.6 us (1%)
    psum x1, waiting for transfers between devices, shards(): fisher_rows = fisher_prior + lax.psum(batch_fisher, 'dp')  644 us
    dot_general x4, matrix products, shards(): lax.dot_general(lax.all_gather(direction, 'tensor', axis=1, tiled=True),...  159 us
    all_gather x4, waiting for transfers between devices, shards(): lax.all_gather(direction, 'tensor', axis=1, tiled=True)  98.9 us
    psum x1, waiting for transfers between devices, shards(): summed = lax.psum(paired, 'tensor')  36.4 us
    add x1, other arithmetic, shards(): fisher_rows = fisher_prior + lax.psum(batch_fisher, 'dp')  33.5 us
    dot_general x1, matrix products, shards(): jnp.dot(own_grads.T, gradients, precision=lax.Precision.HIGHEST)  30.2 us
  transfers between devices with their start and end apart: 7, of which 5 were waited for; matrix products, arithmetic and copies ran while one was open for 6% of the time, Pallas kernels for 0%

commit v1 on v0

v1 whole, which is shorter than its diff:
```python
import jax
import jax.numpy as jnp
from jax import lax
from jax.sharding import PartitionSpec as P

LEN = 512
ITERS = 4
DAMPING = 0.1
CONTRACT = (((1,), (1,)), ((), ()))
HIGH = lax.Precision.HIGH


def shards(activations, out_grads, proj_in, proj_out, fisher_prior, test_grads):
    batch_rows, length_tok, width_ff = activations.shape
    width_model = out_grads.shape[2]
    rank = proj_in.shape[1]
    entries = test_grads.shape[1]
    act_part = jnp.dot(
        activations.reshape(-1, width_ff), proj_in, preferred_element_type=jnp.float32
    ).reshape(batch_rows, length_tok, -1)
    grad_part = jnp.dot(
        out_grads.reshape(-1, width_model), proj_out, preferred_element_type=jnp.float32
    ).reshape(batch_rows, length_tok, -1)
    paired = jnp.concatenate([grad_part, act_part], axis=2)
    summed = lax.psum_scatter(paired, "tensor", scatter_dimension=1, tiled=True)
    products = jnp.einsum(
        "eto,eti->eoi", summed[:, :, :rank], summed[:, :, rank:], precision=HIGH
    )
    partial = products.reshape(batch_rows, entries) / LEN
    pieces = lax.all_gather(partial, ("tensor", "dp"), axis=0, tiled=True)
    gradients = jnp.sum(pieces.reshape(lax.axis_size("tensor"), -1, entries), axis=0)
    rows_here = fisher_prior.shape[0]
    offset = lax.axis_index("tensor") * rows_here
    residual = test_grads
    direction = residual
    solution = jnp.zeros_like(residual)
    norm_now = jnp.sum(residual * residual, axis=1)
    for iteration in range(ITERS):
        image = lax.dot_general(direction, fisher_prior, CONTRACT, precision=HIGH)
        image = lax.all_gather(image, "tensor", axis=1, tiled=True)
        coeffs = lax.dot_general(direction, gradients, CONTRACT, precision=HIGH)
        low = jnp.dot(coeffs, gradients, precision=HIGH)
        applied = image + low + DAMPING * direction
        step_size = norm_now / jnp.sum(direction * applied, axis=1)
        solution = solution + step_size[:, None] * direction
        if iteration + 1 < ITERS:
            residual = residual - step_size[:, None] * applied
            norm_next = jnp.sum(residual * residual, axis=1)
            direction = residual + (norm_next / norm_now)[:, None] * direction
            norm_now = norm_next
    own = lax.dynamic_slice_in_dim(solution, offset, rows_here, 1)
    scores = lax.dot_general(solution, gradients, CONTRACT, precision=HIGH)
    full = lax.all_gather(own, "dp", axis=0, tiled=True)
    table = lax.all_gather(scores, "dp", axis=0, tiled=True)
    start = lax.axis_index("dp") * batch_rows
    return (lax.dynamic_slice_in_dim(table, start, batch_rows, 1).T, full)


def solution(mesh):
    return jax.shard_map(
        shards,
        mesh=mesh,
        in_specs=(
            P(("parts", "dp"), None, "tensor"),
            P(("parts", "dp"), None, "tensor"),
            P("tensor", None),
            P("tensor", None),
            P("tensor", None),
            P(("parts", "dp"), None),
        ),
        out_specs=(P(("parts", "dp"), None), P("parts", "tensor")),
        check_vma=False,
    )
```

time: 1120 us -> 204 us (0.18)
  waiting for transfers between devices: 780 us -> 4.85 us
  matrix products: 221 us -> 110 us
  other arithmetic: 52 us -> 2.23 us
  blocking collectives: 40.4 us -> 66.9 us
    psum x2 -> x0, waiting for transfers between devices: 680 us -> none  [the longest x1 644 us: shards(): fisher_rows = fisher_prior + lax.psum(batch_fisher, 'dp')]
    dot_general x7 -> x14, matrix products: 192 us -> 80.4 us  [the longest x4 76 us: shards(): image = lax.dot_general(direction, fisher_prior, CONTRACT, precision=HIGH)]
    all_gather x5 -> x1, waiting for transfers between devices: 98.9 us -> 4.82 us  [shards(): full = lax.all_gather(own, 'dp', axis=0, tiled=True)]
    all_gather x0 -> x6, blocking collectives: none -> 66.9 us  [the longest x1 27.5 us: shards(): pieces = lax.all_gather(partial, ('tensor', 'dp'), axis=0, tiled=True)]
    psum x8 -> x0, blocking collectives: 40.4 us -> none  [the longest x4 19.9 us: shards(): curve = lax.psum(jnp.sum(direction * applied, axis=1), 'tensor')]
    add x1 -> x0, other arithmetic: 33.5 us -> none  [shards(): fisher_rows = fisher_prior + lax.psum(batch_fisher, 'dp')]
  transfers between devices with their start and end apart: 7 -> 2, of which waited for: 5 -> 1; matrix products, arithmetic and copies ran while one was open for 6% -> 10% of each run, Pallas kernels for 0% -> 0%
where the time goes in v1:
time: 204 us
  matrix products  110 us (54%)
  blocking collectives  66.9 us (33%)
  between operations  14.2 us (7%)
  local copies, waits for them, and re-layouts  5.65 us (3%)
  waiting for transfers between devices  4.85 us (2%)
  other arithmetic  2.23 us (1%)
    dot_general x4, matrix products, shards(): image = lax.dot_general(direction, fisher_prior, CONTRACT, precision=HIGH)  76 us
    all_gather x1, blocking collectives, shards(): pieces = lax.all_gather(partial, ('tensor', 'dp'), axis=0, tiled=True)  27.5 us
    all_gather x4, blocking collectives, shards(): image = lax.all_gather(image, 'tensor', axis=1, tiled=True)  25.4 us
    dot_general x1, matrix products, shards(): jnp.dot(activations.reshape(-1, width_ff), proj_in, preferred_element_typ...  20.8 us
    all_gather x1, blocking collectives, shards(): table = lax.all_gather(scores, 'dp', axis=0, tiled=True)  14 us
    dot_general x1, matrix products, shards(): jnp.dot(out_grads.reshape(-1, width_model), proj_out, preferred_element_t...  8.49 us
    all_gather x1, waiting for transfers between devices, shards(): full = lax.all_gather(own, 'dp', axis=0, tiled=True)  4.82 us
    unnamed x11, local copies, waits for them, and re-layouts  4.5 us
  transfers between devices with their start and end apart: 2, of which 1 were waited for; matrix products, arithmetic and copies ran while one was open for 10% of the time, Pallas kernels for 0%

profile of v1, /device:TPU:0, one launch (start us, length us, event | category | flops | bytes accessed | tf_op | source)
XLA Modules:
  0.0 203.8 jit_solution(4464345828218584701)
XLA Ops:
  7.2 1.4 copy-done
  8.7 20.8 %fusion.5 = f32[3,512,64]{1,2,0:T(8,128)S(1)} fusion(bf16[3,512,14336]{2,1,0:T(8,128)(2,1)} %param.6, bf16[14336,64]{0,1:T(8,128)(2,1)S(1)} %copy-done), kind=kOutput, calls=%fused_computation.9 | convolution fusion | flops 2818572288 | bytes 46268416 | tf_op jit(solution)/shard_map/dot_general | solution.py:18
  29.5 8.5 %fusion.8 = f32[3,512,64]{1,2,0:T(8,128)S(1)} fusion(bf16[3,512,4096]{2,1,0:T(8,128)(2,1)} %param.7, bf16[4096,64]{0,1:T(8,128)(2,1)S(1)} %copy-done.3), kind=kOutput, calls=%fused_computation.14 | convolution fusion | flops 805306368 | bytes 13500416 | tf_op jit(solution)/shard_map/dot_general | solution.py:21
  38.0 0.9 pad_maximum_fusion
  39.2 19.0 %fusion.12 = f32[16,2048]{1,0:T(8,128)S(1)} fusion(f32[16,4096]{1,0:T(8,128)S(1)} %copy-done.2, f32[2048,4096]{1,0:T(8,128)} %param.10), kind=kOutput, calls=%fused_computation.34 | convolution fusion | flops 805306368 | bytes 33947648 | tf_op jit(solution)/shard_map/dot_general | solution.py:39
  58.2 7.1 %all_gather.21 = f32[16,4096]{1,0:T(8,128)S(1)} all-gather(f32[16,2048]{1,0:T(8,128)S(1)} %fusion.12), channel_id=1, replica_groups=mesh['parts'=2,'tensor'=2,'dp'=8] {'tensor'}, dimensions={1}, use_global_device_ids=true | all-gather | bytes 393216 | tf_op jit(solution)/shard_map/all_gather | solution.py:40
  65.3 1.3 convolution_multiply_fusion
  66.7 27.5 %all-gather = f32[16,3,4096]{2,1,0:T(4,128)S(1)} all-gather(f32[1,3,4096]{2,1,0:T(4,128)S(1)} %reshape.54), channel_id=1, replica_groups=mesh['parts'=2,'tensor'=2,'dp'=8] {'tensor','dp'}, dimensions={0}, use_global_device_ids=true | all-gather | bytes 835584 | tf_op jit(solution)/shard_map/all_gather | solution.py:30
  94.2 0.4 reshape.53
  94.7 0.3 fusion.13
  95.0 0.4 multiply_reduce_fusion.5
  95.4 0.2 multiply_reduce_fusion.4
  95.7 19.0 %fusion.14 = f32[16,2048]{1,0:T(8,128)S(1)} fusion(f32[16,4096]{1,0:T(8,128)S(1)} %multiply_add_fusion.3, f32[2048,4096]{1,0:T(8,128)} %param.10), kind=kOutput, calls=%fused_computation.36 | convolution fusion | flops 805306368 | bytes 33947648 | tf_op jit(solution)/shard_map/dot_general | solution.py:39
  114.7 0.3 fusion.15
  115.0 6.7 %all_gather.23 = f32[16,4096]{1,0:T(8,128)S(1)} all-gather(f32[16,2048]{1,0:T(8,128)S(1)} %fusion.14), channel_id=1, replica_groups=mesh['parts'=2,'tensor'=2,'dp'=8] {'tensor'}, dimensions={1}, use_global_device_ids=true | all-gather | bytes 393216 | tf_op jit(solution)/shard_map/all_gather | solution.py:40
  121.7 0.4 multiply_reduce_fusion.3
  122.1 0.3 multiply_reduce_fusion.2
  122.5 19.1 %fusion.16 = f32[16,2048]{1,0:T(8,128)S(1)} fusion(f32[16,4096]{1,0:T(8,128)S(1)} %multiply_add_fusion.2, f32[2048,4096]{1,0:T(8,128)} %param.10), kind=kOutput, calls=%fused_computation.38 | convolution fusion | flops 805306368 | bytes 33947648 | tf_op jit(solution)/shard_map/dot_general | solution.py:39
  141.6 0.3 fusion.17
  141.9 6.0 %all_gather.24 = f32[16,4096]{1,0:T(8,128)S(1)} all-gather(f32[16,2048]{1,0:T(8,128)S(1)} %fusion.16), channel_id=1, replica_groups=mesh['parts'=2,'tensor'=2,'dp'=8] {'tensor'}, dimensions={1}, use_global_device_ids=true | all-gather | bytes 393216 | tf_op jit(solution)/shard_map/all_gather | solution.py:40
  147.9 0.4 multiply_reduce_fusion.1
  148.3 0.2 multiply_reduce_fusion
  148.6 19.0 %fusion.18 = f32[16,2048]{1,0:T(8,128)S(1)} fusion(f32[16,4096]{1,0:T(8,128)S(1)} %multiply_add_fusion.1, f32[2048,4096]{1,0:T(8,128)} %param.10), kind=kOutput, calls=%fused_computation.40 | convolution fusion | flops 805306368 | bytes 33947648 | tf_op jit(solution)/shard_map/dot_general | solution.py:39
  167.6 0.3 fusion.19
  167.9 5.7 %all_gather.25 = f32[16,4096]{1,0:T(8,128)S(1)} all-gather(f32[16,2048]{1,0:T(8,128)S(1)} %fusion.18), channel_id=1, replica_groups=mesh['parts'=2,'tensor'=2,'dp'=8] {'tensor'}, dimensions={1}, use_global_device_ids=true | all-gather | bytes 393216 | tf_op jit(solution)/shard_map/all_gather | solution.py:40
  173.6 0.4 fusion.7
  174.1 0.7 constant_dynamic-slice_fusion
  174.8 0.3 fusion.20
  175.2 14.0 %all_gather.26 = f32[128,24]{1,0:T(8,128)S(1)} all-gather(f32[16,24]{1,0:T(8,128)S(1)} %fusion.20), channel_id=1, replica_groups=mesh['parts'=2,'tensor'=2,'dp'=8] {'dp'}, dimensions={0}, use_global_device_ids=true | all-gather | bytes 13824 | tf_op jit(solution)/shard_map/all_gather | solution.py:54
  189.2 0.7 copy.10
  189.9 4.8 %all-gather.3.cloned.1.call-done = f32[128,2048]{1,0:T(8,128)} async-done(((f32[16,2048]{1,0:T(8,128)}), f32[128,2048]{1,0:T(8,128)}) %all-gather.3.cloned.1.call-update) | async-done | bytes 1048592 | tf_op jit(solution)/shard_map/all_gather | solution.py:53
  194.7 2.3 %copy.12 = f32[128,2048]{1,0:T(8,128)} copy(f32[128,2048]{1,0:T(8,128)} %all-gather.3.cloned.1.call-done) | data formatting | bytes 2097152
  (26 shorter events, 1.1 us)
Async XLA Ops:
  7.2 1.5 copy-start
  7.2 22.3 %copy-start.3 = (bf16[4096,64]{0,1:T(8,128)(2,1)S(1)}, bf16[4096,64]{0,1:T(8,128)(2,1)}, u32[]{:S(2)}) copy-start(bf16[4096,64]{0,1:T(8,128)(2,1)} %param.9) | copy-start | bytes 1572868
  7.2 32.0 %copy-start.2 = (f32[16,4096]{1,0:T(8,128)S(1)}, f32[16,4096]{1,0:T(8,128)}, u32[]{:S(2)}) copy-start(f32[16,4096]{1,0:T(8,128)} %param.11) | copy-start | bytes 786436
  7.2 58.1 %reduce-scatter.2.cloned.1.call-start = ((), (), s32[]{:S(2)}) async-start(), calls=%async_computation.1 | async-start | bytes 1179648 | tf_op jit(solution)/shard_map/reduce_scatter | solution.py:25
  39.0 155.7 %all-gather.3.cloned.1.call-start = ((), (), s32[]{:S(2)}) async-start(), calls=%async_computation.2 | async-start | bytes 1179648 | tf_op jit(solution)/shard_map/all_gather | solution.py:53
  122.4 74.6 %copy-start.1 = (bf16[14336,64]{0,1:T(8,128)(2,1)S(1)}, bf16[14336,64]{0,1:T(8,128)(2,1)}, u32[]{:S(2)}) copy-start(bf16[14336,64]{0,1:T(8,128)(2,1)} %param.8) | copy-start | bytes 5505028
Sparse Core Ops, SparseCore 0:
  39.1 20.1 reduce-scatter.1
  175.0 19.6 all-gather.2

commit v2 on v1

--- a/solution.py
+++ b/solution.py
@@ -1,6 +1,10 @@
+import functools
+
 import jax
 import jax.numpy as jnp
 from jax import lax
+from jax.experimental import pallas as pl
+from jax.experimental.pallas import tpu as pltpu
 from jax.sharding import PartitionSpec as P
 
 LEN = 512
@@ -8,6 +12,288 @@
 DAMPING = 0.1
 CONTRACT = (((1,), (1,)), ((), ()))
 HIGH = lax.Precision.HIGH
+
+LANES = 128
+STAGE = 128
+SLOTS = 4
+CHUNK = 256
+
+
+def split(values):
+    high = values.astype(jnp.bfloat16)
+    return high, (values - high.astype(jnp.float32)).astype(jnp.bfloat16)
+
+
+def dot3(left, right, dims):
+    a_high, a_low = split(left)
+    b_high, b_low = split(right)
+    dot = functools.partial(
+        lax.dot_general, dimension_numbers=dims, preferred_element_type=jnp.float32
+    )
+    return dot(a_high, b_high) + (dot(a_low, b_high) + dot(a_high, b_low))
+
+
+def solve_kernel(
+    groups, examples, prior, grads_in, tests_in, full_out, table_out,
+    high, low, stage, partner_grads, all_grads, grads, tests, residual, direction,
+    solved, images, full, table,
+    stage_sem, pair_send, pair_recv, test_send, test_recv, cast_send, cast_recv,
+    image_send, image_recv, full_send, full_recv, pass_send, pass_recv,
+    table_send, table_recv,
+):
+    x = lax.axis_index("tensor")
+    k = lax.axis_index("dp")
+    z, c = k // 2, lax.rem(k, 2)
+    chips = groups // 2
+    rows, entries = tests_in.shape
+    wide = 2 * rows
+    quarter = high.shape[0]
+    half = 2 * quarter
+    block = grads_in.shape[0]
+    across, sibling = lax.rem(x + 1, 2), z * 2 + lax.rem(c + 1, 2)
+
+    def push(source, target, send, recv, tensor, dp):
+        return pltpu.make_async_remote_copy(
+            src_ref=source, dst_ref=target, send_sem=send, recv_sem=recv,
+            device_id={"tensor": tensor, "dp": dp},
+            device_id_type=pl.DeviceIdType.MESH,
+        )
+
+    quad = [(across, k), (x, sibling), (across, sibling)]
+    far = [(lax.rem(z + step, chips)) for step in range(1, chips)]
+    back = [(lax.rem(z + chips - step, chips)) for step in range(1, chips)]
+
+    def load(index):
+        slot = lax.rem(index, SLOTS)
+        start = pl.multiple_of(c * quarter + index * STAGE, STAGE)
+        return pltpu.make_async_copy(
+            prior.at[pl.ds(start, STAGE), :], stage.at[slot], stage_sem.at[slot]
+        )
+
+    count = quarter // STAGE
+    for index in range(min(SLOTS - 1, count)):
+        load(index).start()
+
+    barrier = pltpu.get_barrier_semaphore()
+    peers = quad + [(x, chip * 2 + core) for chip in far for core in range(2)]
+    for tensor, dp in peers:
+        pl.semaphore_signal(
+            barrier, inc=1, device_id={"tensor": tensor, "dp": dp},
+            device_id_type=pl.DeviceIdType.MESH,
+        )
+    pl.semaphore_wait(barrier, len(peers))
+
+    to_pair = push(grads_in, partner_grads, pair_send, pair_recv, across, k)
+    to_pair.start()
+    mine = tests.at[pl.ds(pl.multiple_of(c * rows, rows), rows), :]
+    other = tests.at[pl.ds(pl.multiple_of((1 - c) * rows, rows), rows), :]
+    to_sibling = push(tests_in, mine, test_send, test_recv, x, sibling)
+    to_sibling.start()
+    mine[...] = tests_in[...]
+
+    own = pl.ds(pl.multiple_of(k * block, 8), block)
+    to_pair.wait()
+    all_grads[own, :] = grads_in[...] + partner_grads[...]
+    casts = []
+    for step in range(1, groups):
+        cast = push(
+            all_grads.at[own, :], all_grads.at[own, :], cast_send.at[step - 1],
+            cast_recv.at[step - 1], x, lax.rem(k + step, groups),
+        )
+        cast.start()
+        casts.append(cast)
+
+    def take(index, carry):
+        @pl.when(index + SLOTS - 1 < count)
+        def _():
+            load(index + SLOTS - 1).start()
+
+        load(index).wait()
+        rows_here = pl.ds(pl.multiple_of(index * STAGE, STAGE), STAGE)
+        part_high, part_low = split(stage[lax.rem(index, SLOTS)])
+        high[rows_here, :] = part_high
+        low[rows_here, :] = part_low
+        return carry
+
+    lax.fori_loop(0, count, take, 0)
+
+    to_sibling.wait_send()
+    push(tests_in, other, test_send, test_recv, x, sibling).wait_recv()
+    start = tests[...]
+    residual[...] = start
+    direction[...] = start
+    solved[...] = jnp.zeros_like(start)
+    norm = jnp.sum(start * start, axis=1, keepdims=True)
+
+    chunks = quarter // CHUNK
+
+    def column(tensor, core, chunk):
+        first = tensor * half + core * quarter + chunk * CHUNK
+        return pl.ds(pl.multiple_of(first, CHUNK), CHUNK)
+
+    def sends(iteration, chunk, send_only=False):
+        area = images.at[iteration, :, column(x, c, chunk)]
+        return [
+            push(area, area, image_send.at[peer, chunk],
+                 image_recv.at[iteration, peer, chunk], *quad[peer])
+            for peer in range(3)
+        ]
+
+    def multiply(iteration):
+        d_high, d_low = split(direction[...])
+        both = jnp.concatenate([d_high, d_low], axis=0)
+
+        def body(chunk, carry):
+            here = pl.ds(pl.multiple_of(chunk * CHUNK, CHUNK), CHUNK)
+            first = lax.dot_general(
+                both, high[here, :], CONTRACT, preferred_element_type=jnp.float32
+            )
+            second = lax.dot_general(
+                d_high, low[here, :], CONTRACT, preferred_element_type=jnp.float32
+            )
+            images[iteration, :, column(x, c, chunk)] = first[:wide] + (
+                first[wide:] + second
+            )
+            for copy in sends(iteration, chunk):
+                copy.start()
+            return carry
+
+        lax.fori_loop(0, chunks, body, 0)
+
+    def finish(iteration):
+        cores = [(across, c), (x, 1 - c), (across, 1 - c)]
+
+        def body(chunk, carry):
+            for peer in range(3):
+                area = images.at[iteration, :, column(*cores[peer], chunk)]
+                push(area, area, image_send.at[peer, chunk],
+                     image_recv.at[iteration, peer, chunk], *quad[peer]).wait_recv()
+            for copy in sends(iteration, chunk):
+                copy.wait_send()
+            return carry
+
+        lax.fori_loop(0, chunks, body, 0)
+
+    def update(iteration, norm):
+        toward = direction[...]
+        coeffs = dot3(toward, grads[...], CONTRACT)
+        shift = dot3(coeffs, grads[...], (((1,), (0,)), ((), ())))
+        finish(iteration)
+        applied = images[iteration] + shift + DAMPING * toward
+        step = norm / jnp.sum(toward * applied, axis=1, keepdims=True)
+        solved[...] = solved[...] + step * toward
+        left = residual[...] - step * applied
+        residual[...] = left
+        fresh = jnp.sum(left * left, axis=1, keepdims=True)
+        direction[...] = left + (fresh / norm) * toward
+        return fresh
+
+    multiply(0)
+    for step in range(1, groups):
+        casts[step - 1].wait_send()
+        source = lax.rem(k + groups - step, groups)
+        area = all_grads.at[pl.ds(pl.multiple_of(source * block, 8), block), :]
+        push(area, area, cast_send.at[step - 1], cast_recv.at[step - 1],
+             x, source).wait_recv()
+    lines = entries // LANES
+    grads[...] = jnp.zeros_like(grads)
+    for line in range(lines):
+        grads[0:examples, line * LANES:(line + 1) * LANES] = all_grads[
+            pl.ds(line, examples, stride=lines), :
+        ]
+    norm = update(0, norm)
+
+    def iterate(iteration, norm):
+        multiply(iteration)
+        return update(iteration, norm)
+
+    lax.fori_loop(1, ITERS, iterate, norm)
+
+    columns = pl.ds(pl.multiple_of(x * half, half), half)
+    ours = solved.at[pl.ds(pl.multiple_of(c * rows, rows), rows), columns]
+    place = lambda group: full.at[pl.ds(pl.multiple_of(group * rows, rows), rows), :]
+    outgoing = []
+    for step in range(chips - 1):
+        copy = push(ours, place(k), full_send.at[step], full_recv.at[step],
+                    x, far[step] * 2 + c)
+        copy.start()
+        outgoing.append(copy)
+    scores = dot3(grads[...], solved[...], CONTRACT)
+    table[z] = jnp.concatenate(
+        [scores, jnp.zeros((scores.shape[0], LANES - wide), jnp.float32)], axis=1
+    )
+    for step in range(chips - 1):
+        copy = push(table.at[z], table.at[z], table_send.at[step],
+                    table_recv.at[step], x, far[step] * 2 + c)
+        copy.start()
+        outgoing.append(copy)
+    full[pl.ds(pl.multiple_of(z * wide, wide), wide), :] = solved[:, columns]
+    for step in range(chips - 1):
+        area = place(back[step] * 2 + c)
+        push(area, area, full_send.at[step], full_recv.at[step],
+             x, back[step] * 2 + c).wait_recv()
+        copy = push(area, area, pass_send.at[step], pass_recv.at[step], x, sibling)
+        copy.start()
+        outgoing.append(copy)
+    for step in range(chips - 1):
+        area = place(back[step] * 2 + (1 - c))
+        push(area, area, pass_send.at[step], pass_recv.at[step],
+             x, sibling).wait_recv()
+        area = table.at[back[step]]
+        push(area, area, table_send.at[step], table_recv.at[step],
+             x, back[step] * 2 + c).wait_recv()
+    for copy in outgoing:
+        copy.wait_send()
+    full_out[...] = full[...]
+    table_out[...] = table[...]
+
+
+def solve(prior, partial, test_grads):
+    groups = lax.axis_size("dp")
+    chips = groups // 2
+    rows, entries = test_grads.shape
+    half = prior.shape[0]
+    quarter = half // 2
+    batch_rows = partial.shape[0] * LANES // entries
+    block = partial.shape[0]
+    examples = groups * batch_rows
+    padded = -(-examples // 16) * 16
+    f32 = jnp.float32
+    vmem = pl.BlockSpec(memory_space=pltpu.VMEM)
+    dma = pltpu.SemaphoreType.DMA
+    chunks = quarter // CHUNK
+    wide = 2 * rows
+    work = pltpu.VMEM((wide, entries), f32)
+    return pl.pallas_call(
+        functools.partial(solve_kernel, groups, examples),
+        out_shape=(
+            jax.ShapeDtypeStruct((groups * rows, half), f32),
+            jax.ShapeDtypeStruct((chips, padded, LANES), f32),
+        ),
+        in_specs=[pl.BlockSpec(memory_space=pl.ANY), vmem, vmem],
+        out_specs=(vmem, vmem),
+        scratch_shapes=[
+            pltpu.VMEM((quarter, entries), jnp.bfloat16),
+            pltpu.VMEM((quarter, entries), jnp.bfloat16),
+            pltpu.VMEM((SLOTS, STAGE, entries), f32),
+            pltpu.VMEM((block, LANES), f32),
+            pltpu.VMEM((groups * block, LANES), f32),
+            pltpu.VMEM((padded, entries), f32),
+            work, work, work, work,
+            pltpu.VMEM((ITERS, wide, entries), f32),
+            pltpu.VMEM((groups * rows, half), f32),
+            pltpu.VMEM((chips, padded, LANES), f32),
+            dma((SLOTS,)), dma, dma, dma, dma,
+            dma((groups - 1,)), dma((groups - 1,)),
+            dma((3, chunks)), dma((ITERS, 3, chunks)),
+            dma((chips - 1,)), dma((chips - 1,)),
+            dma((chips - 1,)), dma((chips - 1,)),
+            dma((chips - 1,)), dma((chips - 1,)),
+        ],
+        compiler_params=pltpu.CompilerParams(
+            collective_id=0, has_side_effects=True, vmem_limit_bytes=56 * 1024 * 1024
+        ),
+    )(prior, partial, test_grads)
 
 
 def shards(activations, out_grads, proj_in, proj_out, fisher_prior, test_grads):
@@ -27,6 +313,12 @@
         "eto,eti->eoi", summed[:, :, :rank], summed[:, :, rank:], precision=HIGH
     )
     partial = products.reshape(batch_rows, entries) / LEN
+    if lax.axis_size("tensor") == 2:
+        full, table = solve(fisher_prior, partial.reshape(-1, LANES), test_grads)
+        start = lax.axis_index("dp") * batch_rows
+        mine = lax.dynamic_slice_in_dim(table, start, batch_rows, 1)
+        mine = mine[:, :, : 2 * test_grads.shape[0]]
+        return (mine.transpose(1, 0, 2).reshape(batch_rows, -1), full)
     pieces = lax.all_gather(partial, ("tensor", "dp"), axis=0, tiled=True)
     gradients = jnp.sum(pieces.reshape(lax.axis_size("tensor"), -1, entries), axis=0)
     rows_here = fisher_prior.shape[0]

time: 204 us -> 136 us (0.67)
  matrix products: 110 us -> 30.6 us
  blocking collectives: 66.9 us -> 0 us
  Pallas kernels: 0 us -> 64.1 us
  waiting for transfers between devices: 4.85 us -> 20.3 us
    dot_general x13 -> x0, matrix products: 79.2 us -> none  [the longest x4 76 us: shards(): image = lax.dot_general(direction, fisher_prior, CONTRACT, precision=HIGH)]
    all_gather x6 -> x0, blocking collectives: 66.9 us -> none  [the longest x1 27.5 us: shards(): pieces = lax.all_gather(partial, ('tensor', 'dp'), axis=0, tiled=True)]
    pallas_call x0 -> x1, Pallas kernels: none -> 64.1 us  [solve(): pl.pallas_call(functools.partial(solve_kernel, groups, examples), out_sha...]
    reduce_scatter x1, waiting for transfers between devices: 0.01 us -> 20.3 us  [shards(): summed = lax.psum_scatter(paired, 'tensor', scatter_dimension=1, tiled=True)]
    all_gather x1 -> x0, waiting for transfers between devices: 4.82 us -> none  [shards(): full = lax.all_gather(own, 'dp', axis=0, tiled=True)]
    unnamed x11 -> x7, local copies, waits for them, and re-layouts: 4.5 us -> 3.75 us
  transfers between devices with their start and end apart: 2 -> 1, of which waited for: 1 -> 1; matrix products, arithmetic and copies ran while one was open for 10% -> 0% of each run, Pallas kernels for 0% -> 0%
where the time goes in v2:
time: 136 us
  Pallas kernels  64.1 us (47%)
  matrix products  30.6 us (22%)
  waiting for transfers between devices  20.3 us (15%)
  between operations  14.1 us (10%)
  local copies, waits for them, and re-layouts  5.9 us (4%)
    pallas_call x1, Pallas kernels, solve(): pl.pallas_call(functools.partial(solve_kernel, groups, examples), out_sha...  64.1 us
    dot_general x1, matrix products, shards(): jnp.dot(activations.reshape(-1, width_ff), proj_in, preferred_element_typ...  20.8 us
    reduce_scatter x1, waiting for transfers between devices, shards(): summed = lax.psum_scatter(paired, 'tensor', scatter_dimension=1, tiled=True)  20.3 us
    dot_general x1, matrix products, shards(): jnp.dot(out_grads.reshape(-1, width_model), proj_out, preferred_element_t...  8.49 us
    unnamed x7, local copies, waits for them, and re-layouts  3.75 us
  transfers between devices with their start and end apart: 1, of which 1 were waited for; matrix products, arithmetic and copies ran while one was open for 0% of the time, Pallas kernels for 0%

profile of v2, /device:TPU:0, one launch (start us, length us, event | category | flops | bytes accessed | tf_op | source)
XLA Modules:
  0.0 136.0 jit_solution(14103315779434168753)
XLA Ops:
  7.2 0.0 copy-start
  7.2 0.0 copy-start.2
  7.2 0.0 reduce-scatter.2.cloned.1.call-start
  7.2 1.4 %copy-done = bf16[14336,64]{0,1:T(8,128)(2,1)S(1)} copy-done((bf16[14336,64]{0,1:T(8,128)(2,1)S(1)}, bf16[14336,64]{0,1:T(8,128)(2,1)}, u32[]{:S(2)}) %copy-start) | copy-done | bytes 1835032
  8.7 20.8 %fusion = f32[3,512,64]{1,2,0:T(8,128)S(1)} fusion(bf16[3,512,14336]{2,1,0:T(8,128)(2,1)} %param.6, bf16[14336,64]{0,1:T(8,128)(2,1)S(1)} %copy-done), kind=kOutput, calls=%fused_computation | convolution fusion | flops 2818572288 | bytes 46268416 | tf_op jit(solution)/shard_map/dot_general | solution.py:304
  29.5 0.0 copy-done.2
  29.5 8.5 %fusion.2 = f32[3,512,64]{1,2,0:T(8,128)S(1)} fusion(bf16[3,512,4096]{2,1,0:T(8,128)(2,1)} %param.7, bf16[4096,64]{0,1:T(8,128)(2,1)S(1)} %copy-done.2), kind=kOutput, calls=%fused_computation.4 | convolution fusion | flops 805306368 | bytes 13500416 | tf_op jit(solution)/shard_map/dot_general | solution.py:307
  38.0 0.9 pad_maximum_fusion
  39.0 0.0 reduce-scatter.2.cloned.1.call-update
  39.0 20.3 %reduce-scatter.2.cloned.1.call-done = f32[3,256,128]{1,2,0:T(8,128)} async-done(((f32[3,512,128]{1,2,0:T(8,128)}), f32[3,256,128]{1,2,0:T(8,128)}) %reduce-scatter.2.cloned.1.call-update) | async-done | bytes 393232 | tf_op jit(solution)/shard_map/reduce_scatter | solution.py:311
  59.3 1.3 convolution_multiply_fusion
  60.5 0.0 copy-start.1
  60.6 0.7 div.10.grads_in
  61.3 64.1 %shard_map.77 = (f32[128,2048]{1,0:T(8,128)}, f32[4,32,128]{2,1,0:T(8,128)}) custom-call(f32[2048,4096]{1,0:T(8,128)} %prior.1, f32[96,128]{1,0:T(8,128)} %div.10.grads_in, f32[16,4096]{1,0:T(8,128)} %tests_in.1), custom_call_target="tpu_custom_call" | custom-call | tf_op jit(solution)/shard_map/pallas_call | solution.py:267
  125.4 0.8 dynamic-slice_bitcast_fusion
  126.2 0.7 reshape.20
  126.9 2.3 %copy.10 = f32[128,2048]{1,0:T(8,128)} copy(f32[128,2048]{1,0:T(8,128)} %get-tuple-element.9) | data formatting | bytes 2097152
  129.2 0.0 copy-done.1
  (1 shorter events, 0.0 us)
Async XLA Ops:
  7.2 1.5 %copy-start = (bf16[14336,64]{0,1:T(8,128)(2,1)S(1)}, bf16[14336,64]{0,1:T(8,128)(2,1)}, u32[]{:S(2)}) copy-start(bf16[14336,64]{0,1:T(8,128)(2,1)} %param.8) | copy-start | bytes 5505028
  7.2 22.3 %copy-start.2 = (bf16[4096,64]{0,1:T(8,128)(2,1)S(1)}, bf16[4096,64]{0,1:T(8,128)(2,1)}, u32[]{:S(2)}) copy-start(bf16[4096,64]{0,1:T(8,128)(2,1)} %param.9) | copy-start | bytes 1572868
  7.2 52.1 %reduce-scatter.2.cloned.1.call-start = ((), (), s32[]{:S(2)}) async-start(), calls=%async_computation.1 | async-start | bytes 1179648 | tf_op jit(solution)/shard_map/reduce_scatter | solution.py:311
  60.5 68.6 %copy-start.1 = (bf16[14336,64]{0,1:T(8,128)(2,1)S(1)}, bf16[14336,64]{0,1:T(8,128)(2,1)}, u32[]{:S(2)}) copy-start(bf16[14336,64]{0,1:T(8,128)(2,1)} %param.8) | copy-start | bytes 5505028
Sparse Core Ops, SparseCore 0:
  39.1 20.1 reduce-scatter.1

commit v3 on v2

--- a/solution.py
+++ b/solution.py
@@ -14,8 +14,9 @@
 HIGH = lax.Precision.HIGH
 
 LANES = 128
-STAGE = 128
+STAGE = 64
 SLOTS = 4
+TOKEN_SLOTS = 3
 CHUNK = 256
 
 
@@ -34,10 +35,12 @@
 
 
 def solve_kernel(
-    groups, examples, prior, grads_in, tests_in, full_out, table_out,
+    groups, examples, length, hidden_in, model_in, prior, basis_in, basis_out, tests_in,
+    full_out, table_out,
+    hidden, model, parts, incoming, mixed, grads_in,
     high, low, stage, partner_grads, all_grads, grads, tests, residual, direction,
     solved, images, full, table,
-    stage_sem, pair_send, pair_recv, test_send, test_recv, cast_send, cast_recv,
+    token_sem, part_send, part_recv, stage_sem, pair_send, pair_recv, test_send, test_recv, cast_send, cast_recv,
     image_send, image_recv, full_send, full_recv, pass_send, pass_recv,
     table_send, table_recv,
 ):
@@ -83,14 +86,83 @@
         )
     pl.semaphore_wait(barrier, len(peers))
 
-    to_pair = push(grads_in, partner_grads, pair_send, pair_recv, across, k)
-    to_pair.start()
     mine = tests.at[pl.ds(pl.multiple_of(c * rows, rows), rows), :]
     other = tests.at[pl.ds(pl.multiple_of((1 - c) * rows, rows), rows), :]
     to_sibling = push(tests_in, mine, test_send, test_recv, x, sibling)
     to_sibling.start()
     mine[...] = tests_in[...]
 
+    batch = parts.shape[0] // 2
+    rank = basis_in.shape[0]
+    span = length // 2
+    steps = 2 * batch
+
+    def fetch(index):
+        turn = index // batch
+        first = (index - turn * batch) * length + lax.rem(across + turn, 2) * span
+        tokens = pl.ds(pl.multiple_of(first, span), span)
+        slot = lax.rem(index, TOKEN_SLOTS)
+        return [
+            pltpu.make_async_copy(
+                hidden_in.at[tokens, :], hidden.at[slot], token_sem.at[0, slot]
+            ),
+            pltpu.make_async_copy(
+                model_in.at[tokens, :], model.at[slot], token_sem.at[1, slot]
+            ),
+        ]
+
+    def pair_part(example):
+        return push(
+            parts.at[example], incoming.at[example], part_send.at[example],
+            part_recv.at[example], across, k,
+        )
+
+    for index in range(min(TOKEN_SLOTS - 1, steps)):
+        for copy in fetch(index):
+            copy.start()
+
+    def project(index, carry):
+        @pl.when(index + TOKEN_SLOTS - 1 < steps)
+        def _():
+            for copy in fetch(index + TOKEN_SLOTS - 1):
+                copy.start()
+
+        for copy in fetch(index):
+            copy.wait()
+        slot = lax.rem(index, TOKEN_SLOTS)
+        parts[index, 0:rank, :] = lax.dot_general(
+            basis_out[...], model[slot], CONTRACT, preferred_element_type=jnp.float32
+        )
+        parts[index, rank:, :] = lax.dot_general(
+            basis_in[...], hidden[slot], CONTRACT, preferred_element_type=jnp.float32
+        )
+
+        @pl.when(index < batch)
+        def _():
+            pair_part(index).start()
+
+        @pl.when(index >= batch)
+        def _():
+            example = index - batch
+            pair_part(example).wait()
+            both = parts[index] + incoming[example]
+            right = both[rank:]
+            mixed[...] = dot3(
+                both[:rank], jnp.concatenate([right, right], axis=0), CONTRACT
+            )
+            pairs = rank // 2
+            even = mixed[pl.ds(0, pairs, stride=2), :]
+            odd = mixed[pl.ds(1, pairs, stride=2), :]
+            lane = lax.broadcasted_iota(jnp.int32, even.shape, 1)
+            grads_in[pl.ds(pl.multiple_of(example * pairs, 8), pairs), :] = (
+                jnp.where(lane < rank, even, odd) / LEN
+            )
+
+        return carry
+
+    lax.fori_loop(0, steps, project, 0)
+    to_pair = push(grads_in, partner_grads, pair_send, pair_recv, across, k)
+    to_pair.start()
     own = pl.ds(pl.multiple_of(k * block, 8), block)
     to_pair.wait()
     all_grads[own, :] = grads_in[...] + partner_grads[...]
@@ -248,14 +320,17 @@
     table_out[...] = table[...]
 
 
-def solve(prior, partial, test_grads):
+def solve(activations, out_grads, proj_in, proj_out, prior, test_grads):
     groups = lax.axis_size("dp")
     chips = groups // 2
     rows, entries = test_grads.shape
     half = prior.shape[0]
     quarter = half // 2
-    batch_rows = partial.shape[0] * LANES // entries
-    block = partial.shape[0]
+    batch_rows, length, width_ff = activations.shape
+    width_model = out_grads.shape[2]
+    rank = proj_in.shape[1]
+    block = batch_rows * entries // LANES
+    span = length // 2
     examples = groups * batch_rows
     padded = -(-examples // 16) * 16
     f32 = jnp.float32
@@ -265,14 +340,20 @@
     wide = 2 * rows
     work = pltpu.VMEM((wide, entries), f32)
     return pl.pallas_call(
-        functools.partial(solve_kernel, groups, examples),
+        functools.partial(solve_kernel, groups, examples, length),
         out_shape=(
             jax.ShapeDtypeStruct((groups * rows, half), f32),
             jax.ShapeDtypeStruct((chips, padded, LANES), f32),
         ),
-        in_specs=[pl.BlockSpec(memory_space=pl.ANY), vmem, vmem],
+        in_specs=[pl.BlockSpec(memory_space=pl.ANY)] * 3 + [vmem] * 3,
         out_specs=(vmem, vmem),
         scratch_shapes=[
+            pltpu.VMEM((TOKEN_SLOTS, span, width_ff), jnp.bfloat16),
+            pltpu.VMEM((TOKEN_SLOTS, span, width_model), jnp.bfloat16),
+            pltpu.VMEM((2 * batch_rows, 2 * rank, span), f32),
+            pltpu.VMEM((batch_rows, 2 * rank, span), f32),
+            pltpu.VMEM((rank, LANES), f32),
+            pltpu.VMEM((block, LANES), f32),
             pltpu.VMEM((quarter, entries), jnp.bfloat16),
             pltpu.VMEM((quarter, entries), jnp.bfloat16),
             pltpu.VMEM((SLOTS, STAGE, entries), f32),
@@ -283,6 +364,7 @@
             pltpu.VMEM((ITERS, wide, entries), f32),
             pltpu.VMEM((groups * rows, half), f32),
             pltpu.VMEM((chips, padded, LANES), f32),
+            dma((2, TOKEN_SLOTS)), dma((batch_rows,)), dma((batch_rows,)),
             dma((SLOTS,)), dma, dma, dma, dma,
             dma((groups - 1,)), dma((groups - 1,)),
             dma((3, chunks)), dma((ITERS, 3, chunks)),
@@ -291,9 +373,12 @@
             dma((chips - 1,)), dma((chips - 1,)),
         ],
         compiler_params=pltpu.CompilerParams(
-            collective_id=0, has_side_effects=True, vmem_limit_bytes=56 * 1024 * 1024
+            collective_id=0, has_side_effects=True, vmem_limit_bytes=62 * 1024 * 1024
         ),
-    )(prior, partial, test_grads)
+    )(
+        activations.reshape(-1, width_ff), out_grads.reshape(-1, width_model), prior,
+        proj_in.T, proj_out.T, test_grads,
+    )
 
 
 def shards(activations, out_grads, proj_in, proj_out, fisher_prior, test_grads):
@@ -301,6 +386,14 @@
     width_model = out_grads.shape[2]
     rank = proj_in.shape[1]
     entries = test_grads.shape[1]
+    if lax.axis_size("tensor") == 2 and 2 * rank == LANES:
+        full, table = solve(
+            activations, out_grads, proj_in, proj_out, fisher_prior, test_grads
+        )
+        start = lax.axis_index("dp") * batch_rows
+        mine = lax.dynamic_slice_in_dim(table, start, batch_rows, 1)
+        mine = mine[:, :, : 2 * test_grads.shape[0]]
+        return (mine.transpose(1, 0, 2).reshape(batch_rows, -1), full)
     act_part = jnp.dot(
         activations.reshape(-1, width_ff), proj_in, preferred_element_type=jnp.float32
     ).reshape(batch_rows, length_tok, -1)
@@ -313,12 +406,6 @@
         "eto,eti->eoi", summed[:, :, :rank], summed[:, :, rank:], precision=HIGH
     )
     partial = products.reshape(batch_rows, entries) / LEN
-    if lax.axis_size("tensor") == 2:
-        full, table = solve(fisher_prior, partial.reshape(-1, LANES), test_grads)
-        start = lax.axis_index("dp") * batch_rows
-        mine = lax.dynamic_slice_in_dim(table, start, batch_rows, 1)
-        mine = mine[:, :, : 2 * test_grads.shape[0]]
-        return (mine.transpose(1, 0, 2).reshape(batch_rows, -1), full)
     pieces = lax.all_gather(partial, ("tensor", "dp"), axis=0, tiled=True)
     gradients = jnp.sum(pieces.reshape(lax.axis_size("tensor"), -1, entries), axis=0)
     rows_here = fisher_prior.shape[0]

time: 136 us -> 95.8 us (0.70)
  matrix products: 30.6 us -> 0 us
  Pallas kernels: 64.1 us -> 91.2 us
  waiting for transfers between devices: 20.3 us -> 0 us
  between operations: 14.1 us -> 0.65 us
  local copies, waits for them, and re-layouts: 5.9 us -> 3.74 us
    dot_general x3 -> x0, matrix products: 30.6 us -> none  [the longest x1 20.8 us: shards(): jnp.dot(activations.reshape(-1, width_ff), proj_in, preferred_element_typ...]
    pallas_call x1, Pallas kernels: 64.1 us -> 91.2 us  [solve(): pl.pallas_call(functools.partial(solve_kernel, groups, examples, length),...]
    reduce_scatter x1 -> x0, waiting for transfers between devices: 20.3 us -> none  [shards(): summed = lax.psum_scatter(paired, 'tensor', scatter_dimension=1, tiled=True)]
    unnamed x7 -> x1, local copies, waits for them, and re-layouts: 3.75 us -> 2.29 us
  transfers between devices with their start and end apart: 1 -> 0, of which waited for: 1 -> 0; matrix products, arithmetic and copies ran while one was open for 0% -> 0% of each run, Pallas kernels for 0% -> 0%
where the time goes in v3:
time: 95.8 us; the launch traced here: 95.6 us
  Pallas kernels  91.2 us (95%)
  local copies, waits for them, and re-layouts  3.74 us (4%)
    pallas_call x1, Pallas kernels, solve(): pl.pallas_call(functools.partial(solve_kernel, groups, examples, length),...  91.2 us
    unnamed x1, local copies, waits for them, and re-layouts  2.29 us

profile of v3, /device:TPU:0, one launch (start us, length us, event | category | flops | bytes accessed | tf_op | source)
XLA Modules:
  0.0 95.6 jit_solution(10252474792090551268)
XLA Ops:
  0.6 91.2 %shard_map.77 = (f32[128,2048]{1,0:T(8,128)}, f32[4,32,128]{2,1,0:T(8,128)}) custom-call(bf16[1536,14336]{1,0:T(8,128)(2,1)} %bitcast.6, bf16[1536,4096]{1,0:T(8,128)(2,1)} %bitcast.7, f32[2048,4096]{1,0:T(8,128)} %prior.1, bf16[64,14336]{1,0:T(8,128)(2,1)} %bitcast.8, bf16[64,4096]{1,0:T(8,128)(2,1)} %bitcast.9, f32[16,4096]{1,0:T(8,128)} %tests_in.1), custom_call_target="tpu_custom_call" | custom-call | tf_op jit(solution)/shard_map/pallas_call | solution.py:342
  91.8 0.8 dynamic-slice_bitcast_fusion
  92.6 0.7 reshape.15
  93.3 2.3 %copy.10 = f32[128,2048]{1,0:T(8,128)} copy(f32[128,2048]{1,0:T(8,128)} %get-tuple-element.9) | data formatting | bytes 2097152
  (1 shorter events, 0.0 us)

commit v4 on v3

--- a/solution.py
+++ b/solution.py
@@ -163,18 +163,6 @@
     lax.fori_loop(0, steps, project, 0)
     to_pair = push(grads_in, partner_grads, pair_send, pair_recv, across, k)
     to_pair.start()
-    own = pl.ds(pl.multiple_of(k * block, 8), block)
-    to_pair.wait()
-    all_grads[own, :] = grads_in[...] + partner_grads[...]
-    casts = []
-    for step in range(1, groups):
-        cast = push(
-            all_grads.at[own, :], all_grads.at[own, :], cast_send.at[step - 1],
-            cast_recv.at[step - 1], x, lax.rem(k + step, groups),
-        )
-        cast.start()
-        casts.append(cast)
-
     def take(index, carry):
         @pl.when(index + SLOTS - 1 < count)
         def _():
@@ -186,8 +174,6 @@
         high[rows_here, :] = part_high
         low[rows_here, :] = part_low
         return carry
-
-    lax.fori_loop(0, count, take, 0)
 
     to_sibling.wait_send()
     push(tests_in, other, test_send, test_recv, x, sibling).wait_recv()
@@ -211,11 +197,13 @@
             for peer in range(3)
         ]
 
-    def multiply(iteration):
+    def multiply(iteration, first_pass=False):
         d_high, d_low = split(direction[...])
         both = jnp.concatenate([d_high, d_low], axis=0)
 
         def body(chunk, carry):
+            if first_pass:
+                lax.fori_loop(chunk * per_chunk, (chunk + 1) * per_chunk, take, 0)
             here = pl.ds(pl.multiple_of(chunk * CHUNK, CHUNK), CHUNK)
             first = lax.dot_general(
                 both, high[here, :], CONTRACT, preferred_element_type=jnp.float32
@@ -230,6 +218,9 @@
                 copy.start()
             return carry
 
+        if first_pass:
+            lax.fori_loop(0, 1, body, 0)
+            return body
         lax.fori_loop(0, chunks, body, 0)
 
     def finish(iteration):
@@ -260,7 +251,21 @@
         direction[...] = left + (fresh / norm) * toward
         return fresh
 
-    multiply(0)
+    per_chunk = CHUNK // STAGE
+    remaining = multiply(0, first_pass=True)
+    own = pl.ds(pl.multiple_of(k * block, 8), block)
+    to_pair.wait()
+    all_grads[own, :] = grads_in[...] + partner_grads[...]
+    casts = []
+    for step in range(1, groups):
+        cast = push(
+            all_grads.at[own, :], all_grads.at[own, :], cast_send.at[step - 1],
+            cast_recv.at[step - 1], x, lax.rem(k + step, groups),
+        )
+        cast.start()
+        casts.append(cast)
+
+    lax.fori_loop(1, chunks, remaining, 0)
     for step in range(1, groups):
         casts[step - 1].wait_send()
         source = lax.rem(k + groups - step, groups)

time: 95.8 us -> 92.3 us (0.963)
  Pallas kernels: 91.2 us -> 87.6 us
    pallas_call x1, Pallas kernels: 91.2 us -> 87.6 us  [solve(): pl.pallas_call(functools.partial(solve_kernel, groups, examples, length),...]
where the time goes in v4:
time: 92.3 us; the launch traced here: 92 us
  Pallas kernels  87.6 us (95%)
  local copies, waits for them, and re-layouts  3.74 us (4%)
    pallas_call x1, Pallas kernels, solve(): pl.pallas_call(functools.partial(solve_kernel, groups, examples, length),...  87.6 us
    unnamed x1, local copies, waits for them, and re-layouts  2.29 us

profile of v4, /device:TPU:0, one launch (start us, length us, event | category | flops | bytes accessed | tf_op | source)
XLA Modules:
  0.0 92.0 jit_solution(16865999536824207756)
XLA Ops:
  0.6 87.6 %shard_map.77 = (f32[128,2048]{1,0:T(8,128)}, f32[4,32,128]{2,1,0:T(8,128)}) custom-call(bf16[1536,14336]{1,0:T(8,128)(2,1)} %bitcast.6, bf16[1536,4096]{1,0:T(8,128)(2,1)} %bitcast.7, f32[2048,4096]{1,0:T(8,128)} %prior.1, bf16[64,14336]{1,0:T(8,128)(2,1)} %bitcast.8, bf16[64,4096]{1,0:T(8,128)(2,1)} %bitcast.9, f32[16,4096]{1,0:T(8,128)} %tests_in.1), custom_call_target="tpu_custom_call" | custom-call | tf_op jit(solution)/shard_map/pallas_call | solution.py:347
  88.2 0.8 dynamic-slice_bitcast_fusion
  89.0 0.7 reshape.15
  89.7 2.3 %copy.10 = f32[128,2048]{1,0:T(8,128)} copy(f32[128,2048]{1,0:T(8,128)} %get-tuple-element.9) | data formatting | bytes 2097152
  (1 shorter events, 0.0 us)
